TPU v7x, 128 devices: a whole 4x4x4 slice. The times are simulated.
128 devices in a mesh: ctx: 16 (over y_hi, z, core), dp: 8 (over x, y_lo).
Axes of the slice: x: 4, y: 4 (y_hi: 2, y_lo: 2; y = y_hi * 2 + y_lo), z: 4, core: 2. Of those that a mesh axis runs over, the one named last changes fastest.
Arguments:
- queries: bfloat16 [16384, 4096], P(('dp', 'ctx')), parts along dimension 0, may hold values from -144 to 144
- keys: bfloat16 [16384, 4096], P(('dp', 'ctx')), parts along dimension 0, may hold values from -6.1 to 6.1
- values: bfloat16 [16384, 4096], P(('dp', 'ctx')), parts along dimension 0, may hold values from -6 to 6
- query_tangent: bfloat16 [16384, 4096], P(('dp', 'ctx')), parts along dimension 0, may hold values from -6 to 6
- key_tangent: bfloat16 [16384, 4096], P(('dp', 'ctx')), parts along dimension 0, may hold values from -6 to 6
- value_tangent: bfloat16 [16384, 4096], P(('dp', 'ctx')), parts along dimension 0, may hold values from -6 to 6
Outputs:
- attended: bfloat16 [16384, 4096], P(('dp', 'ctx')), parts along dimension 0
- attended_tangent: bfloat16 [16384, 4096], P(('dp', 'ctx')), parts along dimension 0
There are 8 independent parts, one for each index of `dp`. A program takes and returns all parts, laid end to end along the dimension named above; each array names one. Nothing has to cross between parts.
All inputs are finite; a program needn't handle non-finite values.
Results may differ from a plain program's by a relative error of at most 0.005.
Values may be sent and summed in bfloat16 or wider, within the bound.
A program may use at most 64 MiB of HBM per device.

v0:
```python
import math

import jax
import jax.numpy as jnp
from jax import lax
from jax.sharding import PartitionSpec as P

HEAD_DIM = 128


def block_scores(query_block, key_heads, factor):
    return (
        jnp.einsum("qhd,khd->hqk", query_block, key_heads, preferred_element_type=jnp.float32)
        * factor
    )


def softmax_rows(scores):
    shifted = jnp.exp(scores - jnp.max(scores, axis=-1, keepdims=True))
    return shifted / jnp.sum(shifted, axis=-1, keepdims=True)


def primal_block(query_block, key_heads, value_heads, factor):
    weights = softmax_rows(block_scores(query_block, key_heads, factor))
    rounded = weights.astype(jnp.bfloat16)
    output = jnp.einsum("hqk,khd->qhd", rounded, value_heads, preferred_element_type=jnp.float32)
    return (output.astype(jnp.bfloat16), weights, rounded)


def tangent_block(
    query_block,
    query_delta,
    key_heads,
    key_delta,
    value_heads,
    value_delta,
    weights,
    rounded,
    factor,
):
    delta = (
        jnp.einsum("qhd,khd->hqk", query_delta, key_heads, preferred_element_type=jnp.float32)
        + jnp.einsum("qhd,khd->hqk", query_block, key_delta, preferred_element_type=jnp.float32)
    ) * factor
    centre = jnp.sum(weights * delta, axis=-1, keepdims=True)
    weight_delta = (weights * (delta - centre)).astype(jnp.bfloat16)
    output_delta = jnp.einsum(
        "hqk,khd->qhd", weight_delta, value_heads, preferred_element_type=jnp.float32
    ) + jnp.einsum("hqk,khd->qhd", rounded, value_delta, preferred_element_type=jnp.float32)
    return output_delta.astype(jnp.bfloat16)


def attend(operands):
    length, single, group, width = operands[0].shape
    flat = tuple((item.reshape(length, single * group, width) for item in operands))
    query_heads, key_heads, value_heads, query_delta, key_delta, value_delta = flat
    heads_here = single * group
    factor = width ** (-0.5)
    block_rows = math.gcd(length, 512)
    count = length // block_rows
    query_blocks = query_heads.reshape(count, block_rows, heads_here, width)
    delta_blocks = query_delta.reshape(count, block_rows, heads_here, width)

    def one_block(inputs):
        query_block, delta_block = inputs
        output, weights, rounded = primal_block(query_block, key_heads, value_heads, factor)
        output_delta = tangent_block(
            query_block,
            delta_block,
            key_heads,
            key_delta,
            value_heads,
            value_delta,
            weights,
            rounded,
            factor,
        )
        return (output, output_delta)

    output, output_delta = lax.map(one_block, (query_blocks, delta_blocks))
    return (
        output.reshape(length, single, group, width),
        output_delta.reshape(length, single, group, width),
    )


def body(queries, keys, values, query_tangent, key_tangent, value_tangent):
    rows_here = queries.shape[0]
    head_count = queries.shape[1] // HEAD_DIM
    groups = lax.axis_size("ctx")
    group = head_count // groups

    def split_heads(array):
        return array.reshape(rows_here, groups, group, HEAD_DIM)

    local = (
        split_heads(queries),
        split_heads(keys),
        split_heads(values),
        split_heads(query_tangent),
        split_heads(key_tangent),
        split_heads(value_tangent),
    )
    primal = (
        lax.all_to_all(local[0], "ctx", split_axis=1, concat_axis=0, tiled=True),
        lax.all_to_all(local[1], "ctx", split_axis=1, concat_axis=0, tiled=True),
        lax.all_to_all(local[2], "ctx", split_axis=1, concat_axis=0, tiled=True),
    )
    tangent = (
        lax.all_to_all(local[3], "ctx", split_axis=1, concat_axis=0, tiled=True),
        lax.all_to_all(local[4], "ctx", split_axis=1, concat_axis=0, tiled=True),
        lax.all_to_all(local[5], "ctx", split_axis=1, concat_axis=0, tiled=True),
    )
    output, output_delta = attend(tuple(primal) + tuple(tangent))
    attended, attended_tangent = (
        lax.all_to_all(output, "ctx", split_axis=0, concat_axis=1, tiled=True),
        lax.all_to_all(output_delta, "ctx", split_axis=0, concat_axis=1, tiled=True),
    )
    return (
        attended.reshape(rows_here, head_count * HEAD_DIM),
        attended_tangent.reshape(rows_here, head_count * HEAD_DIM),
    )


def solution(mesh):
    in_specs = (
        P(("dp", "ctx"), None),
        P(("dp", "ctx"), None),
        P(("dp", "ctx"), None),
        P(("dp", "ctx"), None),
        P(("dp", "ctx"), None),
        P(("dp", "ctx"), None),
    )
    out_specs = (P(("dp", "ctx"), None), P(("dp", "ctx"), None))
    return jax.shard_map(body, mesh=mesh, in_specs=in_specs, out_specs=out_specs, check_vma=False)
```

profile of v0, /device:TPU:1, one launch (start us, length us, event | category | flops | bytes accessed | tf_op | source)
XLA Modules:
  0.0 289.8 jit_solution(9603028975893223265)
XLA Ops:
  3.6 9.5 %all-to-all-start.1 = ((bf16[128,16,2,128]{3,0,2,1:T(8,128)(2,1)}), bf16[128,16,2,128]{3,0,2,1:T(8,128)(2,1)S(1)}, u32[]{:S(2)}, u32[]{:S(2)}) async-start(bf16[128,16,2,128]{3,0,2,1:T(8,128)(2,1)} %copy.55), calls=%async_computation.1 | async-start | bytes 2097152 | tf_op jit(solution)/shard_map/all_to_all | solution.py:106
  16.0 14.3 %all-to-all-done.1 = bf16[128,16,2,128]{3,0,2,1:T(8,128)(2,1)S(1)} async-done(((bf16[128,16,2,128]{3,0,2,1:T(8,128)(2,1)}), bf16[128,16,2,128]{3,0,2,1:T(8,128)(2,1)S(1)}, u32[]{:S(2)}, u32[]{:S(2)}) %all-to-all-start.1) | async-done | bytes 1048608 | tf_op jit(solution)/shard_map/all_to_all | solution.py:106
  30.2 4.4 %all-to-all-start.2 = ((bf16[128,16,2,128]{3,0,2,1:T(8,128)(2,1)}), bf16[128,16,2,128]{3,0,2,1:T(8,128)(2,1)S(1)}, u32[]{:S(2)}, u32[]{:S(2)}) async-start(bf16[128,16,2,128]{3,0,2,1:T(8,128)(2,1)} %copy.58), calls=%async_computation.2 | async-start | bytes 2097152 | tf_op jit(solution)/shard_map/all_to_all | solution.py:107
  37.5 14.4 %all-to-all-done.2 = bf16[128,16,2,128]{3,0,2,1:T(8,128)(2,1)S(1)} async-done(((bf16[128,16,2,128]{3,0,2,1:T(8,128)(2,1)}), bf16[128,16,2,128]{3,0,2,1:T(8,128)(2,1)S(1)}, u32[]{:S(2)}, u32[]{:S(2)}) %all-to-all-start.2) | async-done | bytes 1048608 | tf_op jit(solution)/shard_map/all_to_all | solution.py:107
  51.9 4.4 %all-to-all-start.4 = ((bf16[128,16,2,128]{3,0,2,1:T(8,128)(2,1)}), bf16[128,16,2,128]{3,0,2,1:T(8,128)(2,1)S(1)}, u32[]{:S(2)}, u32[]{:S(2)}) async-start(bf16[128,16,2,128]{3,0,2,1:T(8,128)(2,1)} %copy.63), calls=%async_computation.4 | async-start | bytes 2097152 | tf_op jit(solution)/shard_map/all_to_all | solution.py:111
  56.2 2.3 copy.60
  58.5 15.0 %all-to-all-done.4 = bf16[128,16,2,128]{3,0,2,1:T(8,128)(2,1)S(1)} async-done(((bf16[128,16,2,128]{3,0,2,1:T(8,128)(2,1)}), bf16[128,16,2,128]{3,0,2,1:T(8,128)(2,1)S(1)}, u32[]{:S(2)}, u32[]{:S(2)}) %all-to-all-start.4) | async-done | bytes 1048608 | tf_op jit(solution)/shard_map/all_to_all | solution.py:111
  73.5 5.0 %all-to-all-start.3 = ((bf16[128,16,2,128]{0,3,2,1:T(8,128)(2,1)}), bf16[128,16,2,128]{0,3,2,1:T(8,128)(2,1)}, u32[]{:S(2)}, u32[]{:S(2)}) async-start(bf16[128,16,2,128]{0,3,2,1:T(8,128)(2,1)} %bitcast.116), calls=%async_computation.3 | async-start | bytes 2097152 | tf_op jit(solution)/shard_map/all_to_all | solution.py:110
  78.5 2.3 copy.52
  80.8 15.1 %all-to-all-done.3 = bf16[128,16,2,128]{0,3,2,1:T(8,128)(2,1)} async-done(((bf16[128,16,2,128]{0,3,2,1:T(8,128)(2,1)}), bf16[128,16,2,128]{0,3,2,1:T(8,128)(2,1)}, u32[]{:S(2)}, u32[]{:S(2)}) %all-to-all-start.3) | async-done | bytes 1048608 | tf_op jit(solution)/shard_map/all_to_all | solution.py:110
  95.9 5.0 %all-to-all-start = ((bf16[128,16,2,128]{0,3,2,1:T(8,128)(2,1)}), bf16[128,16,2,128]{0,3,2,1:T(8,128)(2,1)}, u32[]{:S(2)}, u32[]{:S(2)}) async-start(bf16[128,16,2,128]{0,3,2,1:T(8,128)(2,1)} %bitcast.115), calls=%async_computation | async-start | bytes 2097152 | tf_op jit(solution)/shard_map/all_to_all | solution.py:105
  100.9 2.3 copy.65
  103.2 2.3 copy.66
  105.4 12.9 %all-to-all-done = bf16[128,16,2,128]{0,3,2,1:T(8,128)(2,1)} async-done(((bf16[128,16,2,128]{0,3,2,1:T(8,128)(2,1)}), bf16[128,16,2,128]{0,3,2,1:T(8,128)(2,1)}, u32[]{:S(2)}, u32[]{:S(2)}) %all-to-all-start) | async-done | bytes 1048608 | tf_op jit(solution)/shard_map/all_to_all | solution.py:105
  118.3 5.0 %all-to-all-start.5 = ((bf16[128,16,2,128]{3,0,2,1:T(8,128)(2,1)}), bf16[128,16,2,128]{3,0,2,1:T(8,128)(2,1)}, u32[]{:S(2)}, u32[]{:S(2)}) async-start(bf16[128,16,2,128]{3,0,2,1:T(8,128)(2,1)} %copy.66), calls=%async_computation.5 | async-start | bytes 2097152 | tf_op jit(solution)/shard_map/all_to_all | solution.py:112
  124.9 2.3 copy.53
  128.7 2.3 copy.64
  131.0 9.7 %all-to-all-done.5 = bf16[128,16,2,128]{3,0,2,1:T(8,128)(2,1)} async-done(((bf16[128,16,2,128]{3,0,2,1:T(8,128)(2,1)}), bf16[128,16,2,128]{3,0,2,1:T(8,128)(2,1)}, u32[]{:S(2)}, u32[]{:S(2)}) %all-to-all-start.5) | async-done | bytes 1048608 | tf_op jit(solution)/shard_map/all_to_all | solution.py:112
  140.7 2.3 copy.67
  143.0 97.7 %while.12 = (s32[]{:T(128)}, bf16[4,512,2,128]{3,1,0,2:T(8,128)(2,1)}, bf16[4,512,2,128]{3,1,0,2:T(8,128)(2,1)}, bf16[4,512,2,128]{3,1,0,2:T(8,128)(2,1)}, bf16[...) while((s32[]{:T(128)}, ...), condition=%wide.region_4.5_spmd, body=%wide.region_0.4_spmd.sunk | while | flops 3255174144 | bytes 126122176 | solution.py:80
  143.0 6.8 %fusion.94 = (f32[2,512]{1,0:T(2,128)S(1)}, f32[2,512,2048]{2,1,0:T(8,128)}) fusion(bf16[2048,2,128]{2,0,1:T(8,128)(2,1)S(1)} %get-tuple-element.203, bf16[4,512,2,128]{3,1,0,2:T(8,128)(2,1)} %get-tuple-element.202, s32[]{:T(128)} %get-tuple-element.189), kind=kOutput, calls=%fused_computation.38.clone.1 | convolution fusion | flops 543164416 | bytes 9703936 | tf_op jit(solution)/shard_map/while/body/eval_jaxpr/sub | solution.py:19
  151.0 2.5 copy-done.4
  153.5 5.3 %multiply_reduce_fusion.3 = (f32[2,512]{1,0:T(2,128)S(1)}, f32[2,512,2048]{2,1,0:T(8,128)}) fusion(f32[2,512,2048]{2,1,0:T(8,128)S(1)} %copy-done.4, f32[2,512]{1,0:T(2,128)S(1)} %get-tuple-element.176, f32[2,512,2048]{2,1,0:T(8,128)S(1)} %fusion.96, bf16[2048,2,128]{2,0,1:T(8,128)(2,1)S(1)} %copy-done.2, ...), kind=kOutput, calls=%fused_computation.2.clone.1 | convolution fusion | flops 547355648 | bytes 26485248 | tf_op jit(solution)/shard_map/while/body/eval_jaxpr/qhd,khd->hqk/dot_general | solution.py:43
  158.7 4.5 %fusion.97 = f32[2,512,128]{2,1,0:T(8,128)S(1)} fusion(bf16[2048,2,128]{2,0,1:T(8,128)(2,1)S(1)} %get-tuple-element.204, f32[2,512,2048]{2,1,0:T(8,128)} %get-tuple-element.177, f32[2,512]{1,0:T(2,128)S(1)} %get-tuple-element.178, f32[2,512,2048]{2,1,0:T(8,128)S(1)} %copy-done.4, f32[2,512]{1,0:T(2,128)S(1)} %get-tuple-element.176), kind=kOutput, calls=%fused_computation.7.clone.1 | convolution fusion | flops 545259520 | bytes 18358272 | tf_op jit(solution)/shard_map/while/body/eval_jaxpr/hqk,khd->qhd/dot_general | solution.py:47
  163.3 2.1 fusion.98
  165.3 2.1 fusion.95
  167.4 6.7 %fusion.94 = (f32[2,512]{1,0:T(2,128)S(1)}, f32[2,512,2048]{2,1,0:T(8,128)}) fusion(bf16[2048,2,128]{2,0,1:T(8,128)(2,1)S(1)} %get-tuple-element.203, bf16[4,512,2,128]{3,1,0,2:T(8,128)(2,1)} %get-tuple-element.202, s32[]{:T(128)} %get-tuple-element.189), kind=kOutput, calls=%fused_computation.38.clone.1 | convolution fusion | flops 543164416 | bytes 9703936 | tf_op jit(solution)/shard_map/while/body/eval_jaxpr/sub | solution.py:19
  175.4 2.4 copy-done.4
  177.9 5.3 %multiply_reduce_fusion.3 = (f32[2,512]{1,0:T(2,128)S(1)}, f32[2,512,2048]{2,1,0:T(8,128)}) fusion(f32[2,512,2048]{2,1,0:T(8,128)S(1)} %copy-done.4, f32[2,512]{1,0:T(2,128)S(1)} %get-tuple-element.176, f32[2,512,2048]{2,1,0:T(8,128)S(1)} %fusion.96, bf16[2048,2,128]{2,0,1:T(8,128)(2,1)S(1)} %copy-done.2, ...), kind=kOutput, calls=%fused_computation.2.clone.1 | convolution fusion | flops 547355648 | bytes 26485248 | tf_op jit(solution)/shard_map/while/body/eval_jaxpr/qhd,khd->hqk/dot_general | solution.py:43
  183.2 4.5 %fusion.97 = f32[2,512,128]{2,1,0:T(8,128)S(1)} fusion(bf16[2048,2,128]{2,0,1:T(8,128)(2,1)S(1)} %get-tuple-element.204, f32[2,512,2048]{2,1,0:T(8,128)} %get-tuple-element.177, f32[2,512]{1,0:T(2,128)S(1)} %get-tuple-element.178, f32[2,512,2048]{2,1,0:T(8,128)S(1)} %copy-done.4, f32[2,512]{1,0:T(2,128)S(1)} %get-tuple-element.176), kind=kOutput, calls=%fused_computation.7.clone.1 | convolution fusion | flops 545259520 | bytes 18358272 | tf_op jit(solution)/shard_map/while/body/eval_jaxpr/hqk,khd->qhd/dot_general | solution.py:47
  187.7 2.1 fusion.98
  191.9 6.7 %fusion.94 = (f32[2,512]{1,0:T(2,128)S(1)}, f32[2,512,2048]{2,1,0:T(8,128)}) fusion(bf16[2048,2,128]{2,0,1:T(8,128)(2,1)S(1)} %get-tuple-element.203, bf16[4,512,2,128]{3,1,0,2:T(8,128)(2,1)} %get-tuple-element.202, s32[]{:T(128)} %get-tuple-element.189), kind=kOutput, calls=%fused_computation.38.clone.1 | convolution fusion | flops 543164416 | bytes 9703936 | tf_op jit(solution)/shard_map/while/body/eval_jaxpr/sub | solution.py:19
  199.9 2.4 copy-done.4
  202.3 5.3 %multiply_reduce_fusion.3 = (f32[2,512]{1,0:T(2,128)S(1)}, f32[2,512,2048]{2,1,0:T(8,128)}) fusion(f32[2,512,2048]{2,1,0:T(8,128)S(1)} %copy-done.4, f32[2,512]{1,0:T(2,128)S(1)} %get-tuple-element.176, f32[2,512,2048]{2,1,0:T(8,128)S(1)} %fusion.96, bf16[2048,2,128]{2,0,1:T(8,128)(2,1)S(1)} %copy-done.2, ...), kind=kOutput, calls=%fused_computation.2.clone.1 | convolution fusion | flops 547355648 | bytes 26485248 | tf_op jit(solution)/shard_map/while/body/eval_jaxpr/qhd,khd->hqk/dot_general | solution.py:43
  207.6 4.5 %fusion.97 = f32[2,512,128]{2,1,0:T(8,128)S(1)} fusion(bf16[2048,2,128]{2,0,1:T(8,128)(2,1)S(1)} %get-tuple-element.204, f32[2,512,2048]{2,1,0:T(8,128)} %get-tuple-element.177, f32[2,512]{1,0:T(2,128)S(1)} %get-tuple-element.178, f32[2,512,2048]{2,1,0:T(8,128)S(1)} %copy-done.4, f32[2,512]{1,0:T(2,128)S(1)} %get-tuple-element.176), kind=kOutput, calls=%fused_computation.7.clone.1 | convolution fusion | flops 545259520 | bytes 18358272 | tf_op jit(solution)/shard_map/while/body/eval_jaxpr/hqk,khd->qhd/dot_general | solution.py:47
  212.1 2.1 fusion.98
  214.2 2.1 fusion.95
  216.3 6.7 %fusion.94 = (f32[2,512]{1,0:T(2,128)S(1)}, f32[2,512,2048]{2,1,0:T(8,128)}) fusion(bf16[2048,2,128]{2,0,1:T(8,128)(2,1)S(1)} %get-tuple-element.203, bf16[4,512,2,128]{3,1,0,2:T(8,128)(2,1)} %get-tuple-element.202, s32[]{:T(128)} %get-tuple-element.189), kind=kOutput, calls=%fused_computation.38.clone.1 | convolution fusion | flops 543164416 | bytes 9703936 | tf_op jit(solution)/shard_map/while/body/eval_jaxpr/sub | solution.py:19
  224.3 2.4 copy-done.4
  226.8 5.3 %multiply_reduce_fusion.3 = (f32[2,512]{1,0:T(2,128)S(1)}, f32[2,512,2048]{2,1,0:T(8,128)}) fusion(f32[2,512,2048]{2,1,0:T(8,128)S(1)} %copy-done.4, f32[2,512]{1,0:T(2,128)S(1)} %get-tuple-element.176, f32[2,512,2048]{2,1,0:T(8,128)S(1)} %fusion.96, bf16[2048,2,128]{2,0,1:T(8,128)(2,1)S(1)} %copy-done.2, ...), kind=kOutput, calls=%fused_computation.2.clone.1 | convolution fusion | flops 547355648 | bytes 26485248 | tf_op jit(solution)/shard_map/while/body/eval_jaxpr/qhd,khd->hqk/dot_general | solution.py:43
  232.0 4.5 %fusion.97 = f32[2,512,128]{2,1,0:T(8,128)S(1)} fusion(bf16[2048,2,128]{2,0,1:T(8,128)(2,1)S(1)} %get-tuple-element.204, f32[2,512,2048]{2,1,0:T(8,128)} %get-tuple-element.177, f32[2,512]{1,0:T(2,128)S(1)} %get-tuple-element.178, f32[2,512,2048]{2,1,0:T(8,128)S(1)} %copy-done.4, f32[2,512]{1,0:T(2,128)S(1)} %get-tuple-element.176), kind=kOutput, calls=%fused_computation.7.clone.1 | convolution fusion | flops 545259520 | bytes 18358272 | tf_op jit(solution)/shard_map/while/body/eval_jaxpr/hqk,khd->qhd/dot_general | solution.py:47
  236.6 2.1 fusion.98
  240.7 3.6 %copy.71 = bf16[2048,1,2,128]{3,2,1,0:T(2,128)(2,1)} copy(bf16[2048,1,2,128]{3,0,2,1:T(8,128)(2,1)} %bitcast.30) | data formatting | bytes 2097152 | tf_op jit(solution)/shard_map/reshape | solution.py:82
  244.3 4.4 %all-to-all-start.6 = ((bf16[2048,1,2,128]{3,2,1,0:T(2,128)(2,1)}), bf16[2048,1,2,128]{3,2,1,0:T(2,128)(2,1)S(1)}, u32[]{:S(2)}, u32[]{:S(2)}) async-start(bf16[2048,1,2,128]{3,2,1,0:T(2,128)(2,1)} %copy.71), calls=%async_computation.6 | async-start | bytes 2097152 | tf_op jit(solution)/shard_map/all_to_all | solution.py:116
  248.7 3.6 %copy.75 = bf16[2048,1,2,128]{3,2,1,0:T(2,128)(2,1)} copy(bf16[2048,1,2,128]{3,0,2,1:T(8,128)(2,1)} %bitcast.129) | data formatting | bytes 2097152 | tf_op jit(solution)/shard_map/reshape | solution.py:83
  252.3 13.7 %all-to-all-done.6 = bf16[2048,1,2,128]{3,2,1,0:T(2,128)(2,1)S(1)} async-done(((bf16[2048,1,2,128]{3,2,1,0:T(2,128)(2,1)}), bf16[2048,1,2,128]{3,2,1,0:T(2,128)(2,1)S(1)}, u32[]{:S(2)}, u32[]{:S(2)}) %all-to-all-start.6) | async-done | bytes 1048608 | tf_op jit(solution)/shard_map/all_to_all | solution.py:116
  266.0 4.4 %all-to-all-start.7 = ((bf16[2048,1,2,128]{3,2,1,0:T(2,128)(2,1)}), bf16[2048,1,2,128]{3,2,1,0:T(2,128)(2,1)S(1)}, u32[]{:S(2)}, u32[]{:S(2)}) async-start(bf16[2048,1,2,128]{3,2,1,0:T(2,128)(2,1)} %copy.75), calls=%async_computation.7 | async-start | bytes 2097152 | tf_op jit(solution)/shard_map/all_to_all | solution.py:117
  272.5 15.2 %all-to-all-done.7 = bf16[2048,1,2,128]{3,2,1,0:T(2,128)(2,1)S(1)} async-done(((bf16[2048,1,2,128]{3,2,1,0:T(2,128)(2,1)}), bf16[2048,1,2,128]{3,2,1,0:T(2,128)(2,1)S(1)}, u32[]{:S(2)}, u32[]{:S(2)}) %all-to-all-start.7) | async-done | bytes 1048608 | tf_op jit(solution)/shard_map/all_to_all | solution.py:117
  (47 shorter events, 25.2 us)
Async XLA Ops:
  3.6 26.7 %all-to-all-start.1 = ((bf16[128,16,2,128]{3,0,2,1:T(8,128)(2,1)}), bf16[128,16,2,128]{3,0,2,1:T(8,128)(2,1)S(1)}, u32[]{:S(2)}, u32[]{:S(2)}) async-start(bf16[128,16,2,128]{3,0,2,1:T(8,128)(2,1)} %copy.55), calls=%async_computation.1 | async-start | bytes 2097152 | tf_op jit(solution)/shard_map/all_to_all | solution.py:106
  30.2 21.6 %all-to-all-start.2 = ((bf16[128,16,2,128]{3,0,2,1:T(8,128)(2,1)}), bf16[128,16,2,128]{3,0,2,1:T(8,128)(2,1)S(1)}, u32[]{:S(2)}, u32[]{:S(2)}) async-start(bf16[128,16,2,128]{3,0,2,1:T(8,128)(2,1)} %copy.58), calls=%async_computation.2 | async-start | bytes 2097152 | tf_op jit(solution)/shard_map/all_to_all | solution.py:107
  51.9 66.4 %copy-start = (bf16[128,16,2,128]{3,0,2,1:T(8,128)(2,1)}, bf16[128,16,2,128]{3,0,2,1:T(8,128)(2,1)S(1)}, u32[]{:S(2)}) copy-start(bf16[128,16,2,128]{3,0,2,1:T(8,128)(2,1)S(1)} %all-to-all-done.2) | copy-start | bytes 3145732
  51.9 21.7 %all-to-all-start.4 = ((bf16[128,16,2,128]{3,0,2,1:T(8,128)(2,1)}), bf16[128,16,2,128]{3,0,2,1:T(8,128)(2,1)S(1)}, u32[]{:S(2)}, u32[]{:S(2)}) async-start(bf16[128,16,2,128]{3,0,2,1:T(8,128)(2,1)} %copy.63), calls=%async_computation.4 | async-start | bytes 2097152 | tf_op jit(solution)/shard_map/all_to_all | solution.py:111
  73.5 51.4 %copy-start.1 = (bf16[128,16,2,128]{3,0,2,1:T(8,128)(2,1)}, bf16[128,16,2,128]{3,0,2,1:T(8,128)(2,1)S(1)}, u32[]{:S(2)}) copy-start(bf16[128,16,2,128]{3,0,2,1:T(8,128)(2,1)S(1)} %all-to-all-done.4) | copy-start | bytes 3145732
  73.5 22.4 %all-to-all-start.3 = ((bf16[128,16,2,128]{0,3,2,1:T(8,128)(2,1)}), bf16[128,16,2,128]{0,3,2,1:T(8,128)(2,1)}, u32[]{:S(2)}, u32[]{:S(2)}) async-start(bf16[128,16,2,128]{0,3,2,1:T(8,128)(2,1)} %bitcast.116), calls=%async_computation.3 | async-start | bytes 2097152 | tf_op jit(solution)/shard_map/all_to_all | solution.py:110
  95.9 22.4 %all-to-all-start = ((bf16[128,16,2,128]{0,3,2,1:T(8,128)(2,1)}), bf16[128,16,2,128]{0,3,2,1:T(8,128)(2,1)}, u32[]{:S(2)}, u32[]{:S(2)}) async-start(bf16[128,16,2,128]{0,3,2,1:T(8,128)(2,1)} %bitcast.115), calls=%async_computation | async-start | bytes 2097152 | tf_op jit(solution)/shard_map/all_to_all | solution.py:105
  118.3 22.4 %all-to-all-start.5 = ((bf16[128,16,2,128]{3,0,2,1:T(8,128)(2,1)}), bf16[128,16,2,128]{3,0,2,1:T(8,128)(2,1)}, u32[]{:S(2)}, u32[]{:S(2)}) async-start(bf16[128,16,2,128]{3,0,2,1:T(8,128)(2,1)} %copy.66), calls=%async_computation.5 | async-start | bytes 2097152 | tf_op jit(solution)/shard_map/all_to_all | solution.py:112
  149.7 1.3 copy-start.2
  149.7 3.7 %copy-start.4 = (f32[2,512,2048]{2,1,0:T(8,128)S(1)}, f32[2,512,2048]{2,1,0:T(8,128)}, u32[]{:S(2)}) copy-start(f32[2,512,2048]{2,1,0:T(8,128)} %get-tuple-element.175) | copy-start | bytes 25165828 | tf_op jit(solution)/shard_map/while
  158.7 4.5 %copy-start.3 = (bf16[2048,2,128]{2,0,1:T(8,128)(2,1)S(1)}, bf16[2048,2,128]{2,0,1:T(8,128)(2,1)}, u32[]{:S(2)}) copy-start(bf16[2048,2,128]{2,0,1:T(8,128)(2,1)} %get-tuple-element.207) | copy-start | bytes 3145732 | tf_op jit(solution)/shard_map/while
  174.2 1.3 copy-start.2
  174.2 3.7 %copy-start.4 = (f32[2,512,2048]{2,1,0:T(8,128)S(1)}, f32[2,512,2048]{2,1,0:T(8,128)}, u32[]{:S(2)}) copy-start(f32[2,512,2048]{2,1,0:T(8,128)} %get-tuple-element.175) | copy-start | bytes 25165828 | tf_op jit(solution)/shard_map/while
  183.2 4.5 %copy-start.3 = (bf16[2048,2,128]{2,0,1:T(8,128)(2,1)S(1)}, bf16[2048,2,128]{2,0,1:T(8,128)(2,1)}, u32[]{:S(2)}) copy-start(bf16[2048,2,128]{2,0,1:T(8,128)(2,1)} %get-tuple-element.207) | copy-start | bytes 3145732 | tf_op jit(solution)/shard_map/while
  198.6 1.3 copy-start.2
  198.6 3.7 %copy-start.4 = (f32[2,512,2048]{2,1,0:T(8,128)S(1)}, f32[2,512,2048]{2,1,0:T(8,128)}, u32[]{:S(2)}) copy-start(f32[2,512,2048]{2,1,0:T(8,128)} %get-tuple-element.175) | copy-start | bytes 25165828 | tf_op jit(solution)/shard_map/while
  207.6 4.5 %copy-start.3 = (bf16[2048,2,128]{2,0,1:T(8,128)(2,1)S(1)}, bf16[2048,2,128]{2,0,1:T(8,128)(2,1)}, u32[]{:S(2)}) copy-start(bf16[2048,2,128]{2,0,1:T(8,128)(2,1)} %get-tuple-element.207) | copy-start | bytes 3145732 | tf_op jit(solution)/shard_map/while
  223.0 1.3 copy-start.2
  223.0 3.7 %copy-start.4 = (f32[2,512,2048]{2,1,0:T(8,128)S(1)}, f32[2,512,2048]{2,1,0:T(8,128)}, u32[]{:S(2)}) copy-start(f32[2,512,2048]{2,1,0:T(8,128)} %get-tuple-element.175) | copy-start | bytes 25165828 | tf_op jit(solution)/shard_map/while
  232.0 4.5 %copy-start.3 = (bf16[2048,2,128]{2,0,1:T(8,128)(2,1)S(1)}, bf16[2048,2,128]{2,0,1:T(8,128)(2,1)}, u32[]{:S(2)}) copy-start(bf16[2048,2,128]{2,0,1:T(8,128)(2,1)} %get-tuple-element.207) | copy-start | bytes 3145732 | tf_op jit(solution)/shard_map/while
  244.3 21.6 %all-to-all-start.6 = ((bf16[2048,1,2,128]{3,2,1,0:T(2,128)(2,1)}), bf16[2048,1,2,128]{3,2,1,0:T(2,128)(2,1)S(1)}, u32[]{:S(2)}, u32[]{:S(2)}) async-start(bf16[2048,1,2,128]{3,2,1,0:T(2,128)(2,1)} %copy.71), calls=%async_computation.6 | async-start | bytes 2097152 | tf_op jit(solution)/shard_map/all_to_all | solution.py:116
  266.0 21.7 %all-to-all-start.7 = ((bf16[2048,1,2,128]{3,2,1,0:T(2,128)(2,1)}), bf16[2048,1,2,128]{3,2,1,0:T(2,128)(2,1)S(1)}, u32[]{:S(2)}, u32[]{:S(2)}) async-start(bf16[2048,1,2,128]{3,2,1,0:T(2,128)(2,1)} %copy.75), calls=%async_computation.7 | async-start | bytes 2097152 | tf_op jit(solution)/shard_map/all_to_all | solution.py:117
where the time goes:
time: 291 us; the launch traced here: 290 us
  waiting for transfers between devices  110 us (38%)
  matrix products  87.8 us (30%)
  local copies, waits for them, and re-layouts  49.1 us (17%)
  starting transfers between devices  41.8 us (14%)
    sub x4, matrix products, softmax_rows(): shifted = jnp.exp(scores - jnp.max(scores, axis=-1, keepdims=True))  27 us
    dot_general x4, matrix products, tangent_block(): jnp.einsum('qhd,khd->hqk', query_block, key_delta, preferred_element_type...  21.1 us
    dot_general x4, matrix products, tangent_block(): jnp.einsum('hqk,khd->qhd', weight_delta, value_heads, preferred_element_t...  18.1 us
    all_to_all x1, waiting for transfers between devices, body(): lax.all_to_all(output_delta, 'ctx', split_axis=0, concat_axis=1, tiled=True)  15.2 us
    all_to_all x1, waiting for transfers between devices, body(): lax.all_to_all(local[3], 'ctx', split_axis=1, concat_axis=0, tiled=True)  15.1 us
    all_to_all x1, waiting for transfers between devices, body(): lax.all_to_all(local[4], 'ctx', split_axis=1, concat_axis=0, tiled=True)  15 us
    all_to_all x1, waiting for transfers between devices, body(): lax.all_to_all(local[2], 'ctx', split_axis=1, concat_axis=0, tiled=True)  14.4 us
    all_to_all x1, waiting for transfers between devices, body(): lax.all_to_all(local[1], 'ctx', split_axis=1, concat_axis=0, tiled=True)  14.3 us
  transfers between devices with their start and end apart: 8, of which 8 were waited for; matrix products, arithmetic and copies ran while one was open for 10% of the time, Pallas kernels for 0%

commit v1 on v0

v1 whole, which is shorter than its diff:
```python
import functools

import jax
import jax.numpy as jnp
from jax import lax
from jax.experimental import pallas as pl
from jax.experimental.pallas import tpu as pltpu
from jax.sharding import PartitionSpec as P

HEAD_DIM = 128
MESH = pl.DeviceIdType.MESH
Z = 4
CORES = 2
F32 = jnp.float32
BF16 = jnp.bfloat16


def attend(query, query_delta, key, key_delta, value, value_delta):
    factor = HEAD_DIM**-0.5
    across = (((1,), (1,)), ((), ()))
    scores = lax.dot_general(query, key, across, preferred_element_type=F32)
    delta = lax.dot_general(
        jnp.concatenate([query_delta, query], axis=1),
        jnp.concatenate([key, key_delta], axis=1),
        across,
        preferred_element_type=F32,
    )
    top = jnp.max(scores, axis=1, keepdims=True)
    shifted = jnp.exp((scores - top) * factor)
    scale = 1.0 / jnp.sum(shifted, axis=1, keepdims=True)
    centre = jnp.sum(shifted * delta, axis=1, keepdims=True) * scale
    weights = shifted * scale
    weight_delta = (weights * ((delta - centre) * factor)).astype(BF16)
    both = jnp.dot(
        weights.astype(BF16),
        jnp.concatenate([value, value_delta], axis=1),
        preferred_element_type=F32,
    )
    moved = jnp.dot(weight_delta, value, preferred_element_type=F32)
    return both[:, :HEAD_DIM].astype(BF16), (moved + both[:, HEAD_DIM:]).astype(BF16)


def kernel(
    q_in, k_in, v_in, dq_in, dk_in, dv_in,
    out, out_delta,
    kv, qs, res,
    kv_send, kv_recv, q_send, q_recv, o_send, o_recv,
):
    me = lax.axis_index("ctx")
    rows, wide = q_in.shape[0], kv.shape[2]
    n = lax.axis_size("ctx")
    chips = n // CORES
    y_count = chips // Z
    heads = wide // HEAD_DIM
    pair = CORES * rows
    core = lax.rem(me, CORES)
    z = lax.rem(me // CORES, Z)
    y = me // (CORES * Z)

    def chip_at(step, sign):
        dy, dz = step // Z, lax.rem(step, Z)
        there_y = lax.rem(y + sign * dy + y_count, y_count)
        there_z = lax.rem(z + sign * dz + Z, Z)
        return there_y * Z + there_z

    def each_partner(step, act):
        chip = chip_at(step, 1)
        for turn in range(CORES):
            act(chip * CORES + lax.rem(core + turn, CORES))

    def other_core(act):
        for turn in range(1, CORES):
            act(me - core + lax.rem(core + turn, CORES))

    barrier = pltpu.get_barrier_semaphore()

    def greet(device):
        pl.semaphore_signal(barrier, inc=1, device_id={"ctx": device}, device_id_type=MESH)

    other_core(greet)

    def greet_chip(step, carry):
        each_partner(step, greet)
        return carry

    lax.fori_loop(1, chips, greet_chip, 0)
    pl.semaphore_wait(barrier, n - 1)

    mine = pl.ds(pl.multiple_of(me * rows, rows), rows)

    def columns(device):
        return pl.ds(pl.multiple_of(device * wide, wide), wide)

    def send(src, dst, send_sem, recv_sem, device):
        pltpu.make_async_remote_copy(
            src_ref=src, dst_ref=dst, send_sem=send_sem, recv_sem=recv_sem,
            device_id={"ctx": device}, device_id_type=MESH,
        ).start()

    def send_kv(device):
        for i, array in enumerate((k_in, dk_in, v_in, dv_in)):
            send(array.at[:, columns(device)], kv.at[i, mine, :], kv_send, kv_recv, device)

    def send_q(device):
        for i, array in enumerate((q_in, dq_in)):
            send(array.at[:, columns(device)], qs.at[i, mine, :], q_send, q_recv.at[me // CORES], device)

    for i, array in enumerate((k_in, dk_in, v_in, dv_in)):
        pltpu.make_async_copy(array.at[:, columns(me)], kv.at[i, mine, :], kv_recv).start()
    for i, array in enumerate((q_in, dq_in)):
        pltpu.make_async_copy(array.at[:, columns(me)], qs.at[i, mine, :], q_recv.at[me // CORES]).start()

    def kv_chip(i, carry):
        each_partner(chips - i, send_kv)
        return carry

    def q_chip(i, carry):
        each_partner(chips - i, send_q)
        return carry

    other_core(send_kv)
    lax.fori_loop(1, chips, kv_chip, 0)
    other_core(send_q)
    lax.fori_loop(1, chips, q_chip, 0)

    def drain(ref, sem):
        pltpu.make_async_copy(ref, ref, sem).wait()

    drain(kv, kv_recv)

    def finish(chip):
        block = pl.ds(pl.multiple_of(chip * pair, pair), pair)
        drain(qs.at[:, block, :], q_recv.at[chip])
        for head in range(heads):
            lanes = pl.ds(head * HEAD_DIM, HEAD_DIM)
            primal, tangent = attend(
                qs[0, block, lanes], qs[1, block, lanes],
                kv[0, :, lanes], kv[1, :, lanes], kv[2, :, lanes], kv[3, :, lanes],
            )
            res[0, block, lanes] = primal
            res[1, block, lanes] = tangent

    def send_res(device):
        owned = pl.ds(pl.multiple_of(device * rows, rows), rows)
        for i, array in enumerate((out, out_delta)):
            send(res.at[i, owned, :], array.at[:, columns(me)], o_send, o_recv.at[i], device)

    finish(me // CORES)
    for i, array in enumerate((out, out_delta)):
        pltpu.make_async_copy(res.at[i, mine, :], array.at[:, columns(me)], o_recv.at[i]).start()
    other_core(send_res)

    def step_chip(i, carry):
        chip = chip_at(chips - i, -1)
        finish(chip)
        for turn in range(CORES):
            send_res(chip * CORES + lax.rem(core + turn, CORES))
        return carry

    lax.fori_loop(1, chips, step_chip, 0)

    others = pl.ds(0, (n - 1) * rows)
    drain(kv.at[:, others, :], kv_send)
    drain(qs.at[:, others, :], q_send)
    drain(res.at[:, others, :], o_send)
    drain(out, o_recv.at[0])
    drain(out_delta, o_recv.at[1])


def body(*arrays):
    rows, width = arrays[0].shape
    n = lax.axis_size("ctx")
    tokens, wide = rows * n, width // n
    heads = width // HEAD_DIM
    anywhere = pl.BlockSpec(memory_space=pl.ANY)
    dma = pltpu.SemaphoreType.DMA
    products = 6 * 2 * tokens * tokens * HEAD_DIM * heads // n
    return pl.pallas_call(
        kernel,
        out_shape=(jax.ShapeDtypeStruct((rows, width), BF16),) * 2,
        in_specs=[anywhere] * 6,
        out_specs=(anywhere,) * 2,
        scratch_shapes=[
            pltpu.VMEM((4, tokens, wide), BF16),
            pltpu.VMEM((2, tokens, wide), BF16),
            pltpu.VMEM((2, tokens, wide), BF16),
            dma, dma, dma, dma((n // CORES,)), dma, dma((2,)),
        ],
        compiler_params=pltpu.CompilerParams(
            collective_id=0, has_side_effects=True, vmem_limit_bytes=60 << 20
        ),
        cost_estimate=pl.CostEstimate(
            flops=products, bytes_accessed=8 * rows * width * 2, transcendentals=tokens * tokens * heads // n
        ),
        name="attend_exchange",
    )(*arrays)


def solution(mesh):
    spec = P(("dp", "ctx"), None)
    return jax.shard_map(body, mesh=mesh, in_specs=(spec,) * 6, out_specs=(spec,) * 2, check_vma=False)
```

time: 291 us -> 111 us (0.38)
  waiting for transfers between devices: 110 us -> 0 us
  Pallas kernels: 0 us -> 107 us
  matrix products: 87.8 us -> 0 us
  local copies, waits for them, and re-layouts: 49.1 us -> 3.35 us
  starting transfers between devices: 41.8 us -> 0 us
    all_to_all x8 -> x0, waiting for transfers between devices: 110 us -> none  [the longest x1 15.2 us: body(): lax.all_to_all(output_delta, 'ctx', split_axis=0, concat_axis=1, tiled=True)]
    pallas_call x0 -> x1, Pallas kernels: none -> 107 us  [body(): pl.pallas_call(kernel, out_shape=(jax.ShapeDtypeStruct((rows, width), BF1...]
    dot_general x20 -> x0, matrix products: 60.8 us -> none  [the longest x4 21.1 us: tangent_block(): jnp.einsum('qhd,khd->hqk', query_block, key_delta, preferred_element_type...]
    all_to_all x8 -> x0, starting transfers between devices: 41.8 us -> none  [the longest x1 9.46 us: body(): lax.all_to_all(local[1], 'ctx', split_axis=1, concat_axis=0, tiled=True)]
    sub x4 -> x0, matrix products: 27 us -> none  [softmax_rows(): shifted = jnp.exp(scores - jnp.max(scores, axis=-1, keepdims=True))]
    reshape x6 -> x0, local copies, waits for them, and re-layouts: 13.4 us -> none  [the longest x4 6.2 us: split_heads(): return array.reshape(rows_here, groups, group, HEAD_DIM)]
    all_to_all x10 -> x0, local copies, waits for them, and re-layouts: 11.6 us -> none  [the longest x1 2.32 us: body(): lax.all_to_all(local[0], 'ctx', split_axis=1, concat_axis=0, tiled=True)]
    unnamed x12 -> x4, local copies, waits for them, and re-layouts: 14.2 us -> 3.35 us
  transfers between devices with their start and end apart: 8 -> 0, of which waited for: 8 -> 0; matrix products, arithmetic and copies ran while one was open for 10% -> 0% of each run, Pallas kernels for 0% -> 0%
where the time goes in v1:
time: 111 us
  Pallas kernels  107 us (96%)
  local copies, waits for them, and re-layouts  3.35 us (3%)
    pallas_call x1, Pallas kernels, body(): pl.pallas_call(kernel, out_shape=(jax.ShapeDtypeStruct((rows, width), BF1...  107 us
    unnamed x4, local copies, waits for them, and re-layouts  3.35 us

profile of v1, /device:TPU:1, one launch (start us, length us, event | category | flops | bytes accessed | tf_op | source)
XLA Modules:
  0.0 110.8 jit_solution(9245634055723697002)
XLA Ops:
  0.6 106.8 %attend_exchange.1 = (bf16[128,4096]{1,0:T(8,128)(2,1)}, bf16[128,4096]{1,0:T(8,128)(2,1)}) custom-call(bf16[128,4096]{1,0:T(8,128)(2,1)} %q_in.1, bf16[128,4096]{1,0:T(8,128)(2,1)} %k_in.1, bf16[128,4096]{1,0:T(8,128)(2,1)} %v_in.1, bf16[128,4096]{1,0:T(8,128)(2,1)} %dq_in.1, bf16[128,4096]{1,0:T(8,128)(2,1)} %dk_in.1, bf16[128,4096]{1,0:T(8,128)(2,1)} %dv_in.1), custom_call_target="tpu_custom_call" | custom-call | flops 12884901888 | bytes 8388608 | tf_op jit(solution)/shard_map/attend_exchange/pallas_call | solution.py:178
  107.4 0.0 copy-start
  107.4 2.4 %copy.10 = bf16[128,4096]{1,0:T(8,128)(2,1)} copy(bf16[128,4096]{1,0:T(8,128)(2,1)} %get-tuple-element.4) | data formatting | bytes 2097152
  109.8 0.0 copy-done
  109.8 1.0 copy.11
Async XLA Ops:
  107.4 2.4 %copy-start = (bf16[128,4096]{1,0:T(8,128)(2,1)S(1)}, bf16[128,4096]{1,0:T(8,128)(2,1)}, u32[]{:S(2)}) copy-start(bf16[128,4096]{1,0:T(8,128)(2,1)} %get-tuple-element.5) | copy-start | bytes 3145732

commit v2 on v1

v2 whole, which is shorter than its diff:
```python
import functools

import jax
import jax.numpy as jnp
from jax import lax
from jax.experimental import pallas as pl
from jax.experimental.pallas import tpu as pltpu
from jax.sharding import PartitionSpec as P

HEAD_DIM = 128
MESH = pl.DeviceIdType.MESH
Z = 4
CORES = 2
F32 = jnp.float32
BF16 = jnp.bfloat16


def attend(query, query_delta, key, key_delta, value, value_delta):
    factor = HEAD_DIM**-0.5
    across = (((1,), (1,)), ((), ()))
    scores = lax.dot_general(query, key, across, preferred_element_type=F32)
    delta = lax.dot_general(
        jnp.concatenate([query_delta, query], axis=1),
        jnp.concatenate([key, key_delta], axis=1),
        across,
        preferred_element_type=F32,
    )
    top = jnp.max(scores, axis=1, keepdims=True)
    shifted = jnp.exp((scores - top) * factor)
    scale = 1.0 / jnp.sum(shifted, axis=1, keepdims=True)
    centre = jnp.sum(shifted * delta, axis=1, keepdims=True) * scale
    weights = shifted * scale
    weight_delta = (weights * ((delta - centre) * factor)).astype(BF16)
    both = jnp.dot(
        weights.astype(BF16),
        jnp.concatenate([value, value_delta], axis=1),
        preferred_element_type=F32,
    )
    moved = jnp.dot(weight_delta, value, preferred_element_type=F32)
    return both[:, :HEAD_DIM].astype(BF16), (moved + both[:, HEAD_DIM:]).astype(BF16)


def kernel(
    q_in, k_in, v_in, dq_in, dk_in, dv_in,
    out, out_delta,
    kv, qs, res,
    kv_send, kv_recv, q_send, q_recv, o_send, o_recv,
):
    me = lax.axis_index("ctx")
    rows = q_in.shape[0]
    n = lax.axis_size("ctx")
    chips = n // CORES
    y_count = chips // Z
    heads = kv.shape[0]
    wide = heads * HEAD_DIM
    pair = CORES * rows
    core = lax.rem(me, CORES)
    z = lax.rem(me // CORES, Z)
    y = me // (CORES * Z)

    def chip_at(step, sign):
        dy, dz = step // Z, lax.rem(step, Z)
        there_y = lax.rem(y + sign * dy + y_count, y_count)
        there_z = lax.rem(z + sign * dz + Z, Z)
        return there_y * Z + there_z

    def each_partner(step, act):
        chip = chip_at(step, 1)
        for turn in range(CORES):
            act(chip * CORES + lax.rem(core + turn, CORES))

    def other_core(act):
        for turn in range(1, CORES):
            act(me - core + lax.rem(core + turn, CORES))

    barrier = pltpu.get_barrier_semaphore()

    def greet(device):
        pl.semaphore_signal(barrier, inc=1, device_id={"ctx": device}, device_id_type=MESH)

    other_core(greet)

    def greet_chip(step, carry):
        each_partner(step, greet)
        return carry

    lax.fori_loop(1, chips, greet_chip, 0)
    pl.semaphore_wait(barrier, n - 1)

    mine = pl.ds(pl.multiple_of(me * rows, rows), rows)

    def columns(device, head):
        return pl.ds(pl.multiple_of(device * wide + head * HEAD_DIM, HEAD_DIM), HEAD_DIM)

    def send(src, dst, send_sem, recv_sem, device):
        pltpu.make_async_remote_copy(
            src_ref=src, dst_ref=dst, send_sem=send_sem, recv_sem=recv_sem,
            device_id={"ctx": device}, device_id_type=MESH,
        ).start()

    def send_kv(head, device):
        for i, array in enumerate((k_in, dk_in, v_in, dv_in)):
            send(
                array.at[:, columns(device, head)], kv.at[head, i, mine, :],
                kv_send.at[head], kv_recv.at[head], device,
            )

    def send_q(head, device):
        for i, array in enumerate((q_in, dq_in)):
            send(
                array.at[:, columns(device, head)], qs.at[head, i, mine, :],
                q_send.at[head], q_recv.at[head, me // CORES], device,
            )

    def start_head(head, carry):
        for i, array in enumerate((k_in, dk_in, v_in, dv_in)):
            pltpu.make_async_copy(
                array.at[:, columns(me, head)], kv.at[head, i, mine, :], kv_recv.at[head]
            ).start()
        for i, array in enumerate((q_in, dq_in)):
            pltpu.make_async_copy(
                array.at[:, columns(me, head)], qs.at[head, i, mine, :], q_recv.at[head, me // CORES]
            ).start()
        for part in (send_kv, send_q):
            part = functools.partial(part, head)

            def to_chip(i, carry, part=part):
                each_partner(chips - i, part)
                return carry

            other_core(part)
            lax.fori_loop(1, chips, to_chip, 0)
        return carry

    lax.fori_loop(0, heads, start_head, 0)

    def drain(ref, sem):
        pltpu.make_async_copy(ref, ref, sem).wait()

    def send_res(head, device):
        owned = pl.ds(pl.multiple_of(device * rows, rows), rows)
        for i, array in enumerate((out, out_delta)):
            send(res.at[head, i, owned, :], array.at[:, columns(me, head)], o_send, o_recv.at[i], device)

    def step_chip(i, carry):
        head, step = i // chips, lax.rem(i, chips)
        chip = chip_at(lax.rem(chips - step, chips), -1)

        @pl.when(step == 0)
        def _():
            drain(kv.at[head], kv_recv.at[head])

        block = pl.ds(pl.multiple_of(chip * pair, pair), pair)
        drain(qs.at[head, :, block, :], q_recv.at[head, chip])
        primal, tangent = attend(
            qs[head, 0, block, :], qs[head, 1, block, :],
            kv[head, 0], kv[head, 1], kv[head, 2], kv[head, 3],
        )
        res[head, 0, block, :] = primal
        res[head, 1, block, :] = tangent

        @pl.when(step == 0)
        def _():
            for j, array in enumerate((out, out_delta)):
                pltpu.make_async_copy(
                    res.at[head, j, mine, :], array.at[:, columns(me, head)], o_recv.at[j]
                ).start()
            other_core(functools.partial(send_res, head))

        @pl.when(step != 0)
        def _():
            for turn in range(CORES):
                send_res(head, chip * CORES + lax.rem(core + turn, CORES))

        return carry

    lax.fori_loop(0, heads * chips, step_chip, 0)

    others = pl.ds(0, (n - 1) * rows)
    for head in range(heads):
        drain(kv.at[head, :, others, :], kv_send.at[head])
        drain(qs.at[head, :, others, :], q_send.at[head])
    drain(res.at[:, :, others, :], o_send)
    drain(out, o_recv.at[0])
    drain(out_delta, o_recv.at[1])


def body(*arrays):
    rows, width = arrays[0].shape
    n = lax.axis_size("ctx")
    tokens = rows * n
    heads = width // HEAD_DIM // n
    anywhere = pl.BlockSpec(memory_space=pl.ANY)
    dma = pltpu.SemaphoreType.DMA
    products = 6 * 2 * tokens * tokens * HEAD_DIM * heads
    return pl.pallas_call(
        kernel,
        out_shape=(jax.ShapeDtypeStruct((rows, width), BF16),) * 2,
        in_specs=[anywhere] * 6,
        out_specs=(anywhere,) * 2,
        scratch_shapes=[
            pltpu.VMEM((heads, 4, tokens, HEAD_DIM), BF16),
            pltpu.VMEM((heads, 2, tokens, HEAD_DIM), BF16),
            pltpu.VMEM((heads, 2, tokens, HEAD_DIM), BF16),
            dma((heads,)), dma((heads,)), dma((heads,)), dma((heads, n // CORES)), dma, dma((2,)),
        ],
        compiler_params=pltpu.CompilerParams(
            collective_id=0, has_side_effects=True, vmem_limit_bytes=60 << 20
        ),
        cost_estimate=pl.CostEstimate(
            flops=products, bytes_accessed=8 * rows * width * 2, transcendentals=tokens * tokens * heads
        ),
        name="attend_exchange",
    )(*arrays)


def solution(mesh):
    spec = P(("dp", "ctx"), None)
    return jax.shard_map(body, mesh=mesh, in_specs=(spec,) * 6, out_specs=(spec,) * 2, check_vma=False)
```

time: 111 us -> 105 us (0.946)
  Pallas kernels: 107 us -> 101 us
    pallas_call x1, Pallas kernels: 107 us -> 101 us  [body(): pl.pallas_call(kernel, out_shape=(jax.ShapeDtypeStruct((rows, width), BF1...]
where the time goes in v2:
time: 105 us
  Pallas kernels  101 us (96%)
  local copies, waits for them, and re-layouts  3.35 us (3%)
    pallas_call x1, Pallas kernels, body(): pl.pallas_call(kernel, out_shape=(jax.ShapeDtypeStruct((rows, width), BF1...  101 us
    unnamed x4, local copies, waits for them, and re-layouts  3.35 us

profile of v2, /device:TPU:1, one launch (start us, length us, event | category | flops | bytes accessed | tf_op | source)
XLA Modules:
  0.0 105.3 jit_solution(3626324801671661015)
XLA Ops:
  0.6 101.3 %attend_exchange.1 = (bf16[128,4096]{1,0:T(8,128)(2,1)}, bf16[128,4096]{1,0:T(8,128)(2,1)}) custom-call(bf16[128,4096]{1,0:T(8,128)(2,1)} %q_in.1, bf16[128,4096]{1,0:T(8,128)(2,1)} %k_in.1, bf16[128,4096]{1,0:T(8,128)(2,1)} %v_in.1, bf16[128,4096]{1,0:T(8,128)(2,1)} %dq_in.1, bf16[128,4096]{1,0:T(8,128)(2,1)} %dk_in.1, bf16[128,4096]{1,0:T(8,128)(2,1)} %dv_in.1), custom_call_target="tpu_custom_call" | custom-call | flops 12884901888 | bytes 8388608 | tf_op jit(solution)/shard_map/attend_exchange/pallas_call | solution.py:196
  101.9 0.0 copy-start
  101.9 2.4 %copy.10 = bf16[128,4096]{1,0:T(8,128)(2,1)} copy(bf16[128,4096]{1,0:T(8,128)(2,1)} %get-tuple-element.4) | data formatting | bytes 2097152
  104.3 0.0 copy-done
  104.3 1.0 copy.11
Async XLA Ops:
  101.9 2.4 %copy-start = (bf16[128,4096]{1,0:T(8,128)(2,1)S(1)}, bf16[128,4096]{1,0:T(8,128)(2,1)}, u32[]{:S(2)}) copy-start(bf16[128,4096]{1,0:T(8,128)(2,1)} %get-tuple-element.5) | copy-start | bytes 3145732

commit v3 on v2

--- a/solution.py
+++ b/solution.py
@@ -58,14 +58,14 @@
     z = lax.rem(me // CORES, Z)
     y = me // (CORES * Z)
 
-    def chip_at(step, sign):
+    def chip_at(step, sign, way):
         dy, dz = step // Z, lax.rem(step, Z)
         there_y = lax.rem(y + sign * dy + y_count, y_count)
-        there_z = lax.rem(z + sign * dz + Z, Z)
+        there_z = lax.rem(z + sign * way * dz + Z, Z)
         return there_y * Z + there_z
 
     def each_partner(step, act):
-        chip = chip_at(step, 1)
+        chip = chip_at(step, 1, 1 - 2 * core)
         for turn in range(CORES):
             act(chip * CORES + lax.rem(core + turn, CORES))
 
@@ -98,38 +98,25 @@
             device_id={"ctx": device}, device_id_type=MESH,
         ).start()
 
-    def send_kv(head, device):
-        for i, array in enumerate((k_in, dk_in, v_in, dv_in)):
-            send(
-                array.at[:, columns(device, head)], kv.at[head, i, mine, :],
-                kv_send.at[head], kv_recv.at[head], device,
-            )
-
-    def send_q(head, device):
-        for i, array in enumerate((q_in, dq_in)):
-            send(
-                array.at[:, columns(device, head)], qs.at[head, i, mine, :],
-                q_send.at[head], q_recv.at[head, me // CORES], device,
-            )
-
     def start_head(head, carry):
-        for i, array in enumerate((k_in, dk_in, v_in, dv_in)):
-            pltpu.make_async_copy(
-                array.at[:, columns(me, head)], kv.at[head, i, mine, :], kv_recv.at[head]
-            ).start()
-        for i, array in enumerate((q_in, dq_in)):
-            pltpu.make_async_copy(
-                array.at[:, columns(me, head)], qs.at[head, i, mine, :], q_recv.at[head, me // CORES]
-            ).start()
-        for part in (send_kv, send_q):
-            part = functools.partial(part, head)
-
-            def to_chip(i, carry, part=part):
-                each_partner(chips - i, part)
-                return carry
-
-            other_core(part)
-            lax.fori_loop(1, chips, to_chip, 0)
+        groups = (
+            (kv, (k_in, dk_in, v_in, dv_in), kv_send.at[head], kv_recv.at[head]),
+            (qs, (q_in, dq_in), q_send.at[head], q_recv.at[head, me // CORES]),
+        )
+        for buffer, arrays, send_sem, recv_sem in groups:
+            for i, array in enumerate(arrays):
+                there = buffer.at[head, i, mine, :]
+                pltpu.make_async_copy(array.at[:, columns(me, head)], there, recv_sem).start()
+
+                def to_device(device, array=array, there=there, send_sem=send_sem, recv_sem=recv_sem):
+                    send(array.at[:, columns(device, head)], there, send_sem, recv_sem, device)
+
+                def to_chip(i, carry, act=to_device):
+                    each_partner(chips - i, act)
+                    return carry
+
+                other_core(to_device)
+                lax.fori_loop(1, chips, to_chip, 0)
         return carry
 
     lax.fori_loop(0, heads, start_head, 0)
@@ -144,7 +131,7 @@
 
     def step_chip(i, carry):
         head, step = i // chips, lax.rem(i, chips)
-        chip = chip_at(lax.rem(chips - step, chips), -1)
+        chip = chip_at(lax.rem(chips - step, chips), -1, 1)
 
         @pl.when(step == 0)
         def _():
@@ -185,6 +172,26 @@
     drain(out_delta, o_recv.at[1])
 
 
+def settle_kernel(a, b, out_a, out_b, sems):
+    copies = [pltpu.make_async_copy(a, out_a, sems.at[0]), pltpu.make_async_copy(b, out_b, sems.at[1])]
+    for copy in copies:
+        copy.start()
+    for copy in copies:
+        copy.wait()
+
+
+def settle(a, b, space):
+    anywhere = pl.BlockSpec(memory_space=pl.ANY)
+    return pl.pallas_call(
+        settle_kernel,
+        out_shape=(jax.ShapeDtypeStruct(a.shape, a.dtype),) * 2,
+        in_specs=[space] * 2,
+        out_specs=(anywhere,) * 2,
+        scratch_shapes=[pltpu.SemaphoreType.DMA((2,))],
+        name="settle",
+    )(a, b)
+
+
 def body(*arrays):
     rows, width = arrays[0].shape
     n = lax.axis_size("ctx")
@@ -193,11 +200,11 @@
     anywhere = pl.BlockSpec(memory_space=pl.ANY)
     dma = pltpu.SemaphoreType.DMA
     products = 6 * 2 * tokens * tokens * HEAD_DIM * heads
-    return pl.pallas_call(
+    result = pl.pallas_call(
         kernel,
-        out_shape=(jax.ShapeDtypeStruct((rows, width), BF16),) * 2,
+        out_shape=(pltpu.VMEM((rows, width), BF16),) * 2,
         in_specs=[anywhere] * 6,
-        out_specs=(anywhere,) * 2,
+        out_specs=(pl.BlockSpec(memory_space=pltpu.VMEM),) * 2,
         scratch_shapes=[
             pltpu.VMEM((heads, 4, tokens, HEAD_DIM), BF16),
             pltpu.VMEM((heads, 2, tokens, HEAD_DIM), BF16),
@@ -212,6 +219,8 @@
         ),
         name="attend_exchange",
     )(*arrays)
+    result = [pltpu.with_memory_space_constraint(r, pltpu.VMEM) for r in result]
+    return settle(*result, pl.BlockSpec(memory_space=pltpu.VMEM))
 
 
 def solution(mesh):

time: 105 us -> 103 us (0.981)
  local copies, waits for them, and re-layouts: 3.35 us -> 0 us
    unnamed x4 -> x0, local copies, waits for them, and re-layouts: 3.35 us -> none
    pallas_call x1 -> x2, Pallas kernels: 101 us -> 102 us  [the longest x1 101 us: body(): pl.pallas_call(kernel, out_shape=(pltpu.VMEM((rows, width), BF16),) * 2,...]
where the time goes in v3:
time: 103 us
  Pallas kernels  102 us (99%)
    pallas_call x1, Pallas kernels, body(): pl.pallas_call(kernel, out_shape=(pltpu.VMEM((rows, width), BF16),) * 2,...  101 us

profile of v3, /device:TPU:1, one launch (start us, length us, event | category | flops | bytes accessed | tf_op | source)
XLA Modules:
  0.0 102.6 jit_solution(1317358969460578795)
XLA Ops:
  0.6 100.6 %attend_exchange.1 = (bf16[128,4096]{1,0:T(8,128)(2,1)S(1)}, bf16[128,4096]{1,0:T(8,128)(2,1)S(1)}) custom-call(bf16[128,4096]{1,0:T(8,128)(2,1)} %q_in.1, bf16[128,4096]{1,0:T(8,128)(2,1)} %k_in.1, bf16[128,4096]{1,0:T(8,128)(2,1)} %v_in.1, bf16[128,4096]{1,0:T(8,128)(2,1)} %dq_in.1, bf16[128,4096]{1,0:T(8,128)(2,1)} %dk_in.1, bf16[128,4096]{1,0:T(8,128)(2,1)} %dv_in.1), custom_call_target="tpu_custom_call" | custom-call | flops 12884901888 | bytes 8388608 | tf_op jit(solution)/shard_map/attend_exchange/pallas_call | solution.py:203
  101.3 1.3 %settle.1 = (bf16[128,4096]{1,0:T(8,128)(2,1)}, bf16[128,4096]{1,0:T(8,128)(2,1)}) custom-call(bf16[128,4096]{1,0:T(8,128)(2,1)S(1)} %get-tuple-element.4.a, bf16[128,4096]{1,0:T(8,128)(2,1)S(1)} %get-tuple-element.5.b), custom_call_target="tpu_custom_call" | custom-call | tf_op jit(solution)/shard_map/settle/pallas_call | solution.py:185

commit v4 on v3

--- a/solution.py
+++ b/solution.py
@@ -1,4 +1,5 @@
 import functools
+import math
 
 import jax
 import jax.numpy as jnp
@@ -8,6 +9,7 @@
 from jax.sharding import PartitionSpec as P
 
 HEAD_DIM = 128
+LOG2_E = math.log2(math.e)
 MESH = pl.DeviceIdType.MESH
 Z = 4
 CORES = 2
@@ -15,28 +17,21 @@
 BF16 = jnp.bfloat16
 
 
-def attend(query, query_delta, key, key_delta, value, value_delta):
+def attend(queries, keys, values):
     factor = HEAD_DIM**-0.5
     across = (((1,), (1,)), ((), ()))
-    scores = lax.dot_general(query, key, across, preferred_element_type=F32)
-    delta = lax.dot_general(
-        jnp.concatenate([query_delta, query], axis=1),
-        jnp.concatenate([key, key_delta], axis=1),
-        across,
-        preferred_element_type=F32,
+    scores = lax.dot_general(
+        queries[:, HEAD_DIM:], keys[:, :HEAD_DIM], across, preferred_element_type=F32
     )
+    delta = lax.dot_general(queries, keys, across, preferred_element_type=F32)
     top = jnp.max(scores, axis=1, keepdims=True)
-    shifted = jnp.exp((scores - top) * factor)
+    shifted = jnp.exp2((scores - top) * (factor * LOG2_E))
     scale = 1.0 / jnp.sum(shifted, axis=1, keepdims=True)
     centre = jnp.sum(shifted * delta, axis=1, keepdims=True) * scale
     weights = shifted * scale
     weight_delta = (weights * ((delta - centre) * factor)).astype(BF16)
-    both = jnp.dot(
-        weights.astype(BF16),
-        jnp.concatenate([value, value_delta], axis=1),
-        preferred_element_type=F32,
-    )
-    moved = jnp.dot(weight_delta, value, preferred_element_type=F32)
+    both = jnp.dot(weights.astype(BF16), values, preferred_element_type=F32)
+    moved = jnp.dot(weight_delta, values[:, :HEAD_DIM], preferred_element_type=F32)
     return both[:, :HEAD_DIM].astype(BF16), (moved + both[:, HEAD_DIM:]).astype(BF16)
 
 
@@ -51,7 +46,7 @@
     n = lax.axis_size("ctx")
     chips = n // CORES
     y_count = chips // Z
-    heads = kv.shape[0]
+    heads = res.shape[0]
     wide = heads * HEAD_DIM
     pair = CORES * rows
     core = lax.rem(me, CORES)
@@ -78,13 +73,9 @@
     def greet(device):
         pl.semaphore_signal(barrier, inc=1, device_id={"ctx": device}, device_id_type=MESH)
 
+    for step in range(chips - 1, 0, -1):
+        each_partner(step, greet)
     other_core(greet)
-
-    def greet_chip(step, carry):
-        each_partner(step, greet)
-        return carry
-
-    lax.fori_loop(1, chips, greet_chip, 0)
     pl.semaphore_wait(barrier, n - 1)
 
     mine = pl.ds(pl.multiple_of(me * rows, rows), rows)
@@ -100,12 +91,12 @@
 
     def start_head(head, carry):
         groups = (
-            (kv, (k_in, dk_in, v_in, dv_in), kv_send.at[head], kv_recv.at[head]),
-            (qs, (q_in, dq_in), q_send.at[head], q_recv.at[head, me // CORES]),
+            ((k_in, dk_in, v_in, dv_in), (kv.at[head, 0], kv.at[head, 1]), kv_send.at[head], kv_recv.at[head]),
+            ((dq_in, q_in), (qs.at[head],), q_send.at[head], q_recv.at[head, me // CORES]),
         )
-        for buffer, arrays, send_sem, recv_sem in groups:
+        for arrays, pairs, send_sem, recv_sem in groups:
             for i, array in enumerate(arrays):
-                there = buffer.at[head, i, mine, :]
+                there = pairs[i // 2].at[mine, pl.ds(i % 2 * HEAD_DIM, HEAD_DIM)]
                 pltpu.make_async_copy(array.at[:, columns(me, head)], there, recv_sem).start()
 
                 def to_device(device, array=array, there=there, send_sem=send_sem, recv_sem=recv_sem):
@@ -131,18 +122,15 @@
 
     def step_chip(i, carry):
         head, step = i // chips, lax.rem(i, chips)
-        chip = chip_at(lax.rem(chips - step, chips), -1, 1)
+        chip = chip_at(lax.rem(chips - step, chips), -1, 1 - 2 * core)
 
         @pl.when(step == 0)
         def _():
             drain(kv.at[head], kv_recv.at[head])
 
         block = pl.ds(pl.multiple_of(chip * pair, pair), pair)
-        drain(qs.at[head, :, block, :], q_recv.at[head, chip])
-        primal, tangent = attend(
-            qs[head, 0, block, :], qs[head, 1, block, :],
-            kv[head, 0], kv[head, 1], kv[head, 2], kv[head, 3],
-        )
+        drain(qs.at[head, block, :], q_recv.at[head, chip])
+        primal, tangent = attend(qs[head, block, :], kv[head, 0], kv[head, 1])
         res[head, 0, block, :] = primal
         res[head, 1, block, :] = tangent
 
@@ -166,7 +154,7 @@
     others = pl.ds(0, (n - 1) * rows)
     for head in range(heads):
         drain(kv.at[head, :, others, :], kv_send.at[head])
-        drain(qs.at[head, :, others, :], q_send.at[head])
+        drain(qs.at[head, others, :], q_send.at[head])
     drain(res.at[:, :, others, :], o_send)
     drain(out, o_recv.at[0])
     drain(out_delta, o_recv.at[1])
@@ -206,8 +194,8 @@
         in_specs=[anywhere] * 6,
         out_specs=(pl.BlockSpec(memory_space=pltpu.VMEM),) * 2,
         scratch_shapes=[
-            pltpu.VMEM((heads, 4, tokens, HEAD_DIM), BF16),
-            pltpu.VMEM((heads, 2, tokens, HEAD_DIM), BF16),
+            pltpu.VMEM((heads, 2, tokens, 2 * HEAD_DIM), BF16),
+            pltpu.VMEM((heads, tokens, 2 * HEAD_DIM), BF16),
             pltpu.VMEM((heads, 2, tokens, HEAD_DIM), BF16),
             dma((heads,)), dma((heads,)), dma((heads,)), dma((heads, n // CORES)), dma, dma((2,)),
         ],

time: 103 us -> 102 us (level)
  no operation moved by 1% of the time
where the time goes in v4:
time: 102 us
  Pallas kernels  101 us (99%)
    pallas_call x1, Pallas kernels, body(): pl.pallas_call(kernel, out_shape=(pltpu.VMEM((rows, width), BF16),) * 2,...  100 us

profile of v4, /device:TPU:1, one launch (start us, length us, event | category | flops | bytes accessed | tf_op | source)
XLA Modules:
  0.0 102.1 jit_solution(7519075854819803189)
XLA Ops:
  0.6 100.1 %attend_exchange.1 = (bf16[128,4096]{1,0:T(8,128)(2,1)S(1)}, bf16[128,4096]{1,0:T(8,128)(2,1)S(1)}) custom-call(bf16[128,4096]{1,0:T(8,128)(2,1)} %q_in.1, bf16[128,4096]{1,0:T(8,128)(2,1)} %k_in.1, bf16[128,4096]{1,0:T(8,128)(2,1)} %v_in.1, bf16[128,4096]{1,0:T(8,128)(2,1)} %dq_in.1, bf16[128,4096]{1,0:T(8,128)(2,1)} %dk_in.1, bf16[128,4096]{1,0:T(8,128)(2,1)} %dv_in.1), custom_call_target="tpu_custom_call" | custom-call | flops 12884901888 | bytes 8388608 | tf_op jit(solution)/shard_map/attend_exchange/pallas_call | solution.py:191
  100.7 1.3 %settle.1 = (bf16[128,4096]{1,0:T(8,128)(2,1)}, bf16[128,4096]{1,0:T(8,128)(2,1)}) custom-call(bf16[128,4096]{1,0:T(8,128)(2,1)S(1)} %get-tuple-element.4.a, bf16[128,4096]{1,0:T(8,128)(2,1)S(1)} %get-tuple-element.5.b), custom_call_target="tpu_custom_call" | custom-call | tf_op jit(solution)/shard_map/settle/pallas_call | solution.py:173

commit v5 on v4

--- a/solution.py
+++ b/solution.py
@@ -97,7 +97,6 @@
         for arrays, pairs, send_sem, recv_sem in groups:
             for i, array in enumerate(arrays):
                 there = pairs[i // 2].at[mine, pl.ds(i % 2 * HEAD_DIM, HEAD_DIM)]
-                pltpu.make_async_copy(array.at[:, columns(me, head)], there, recv_sem).start()
 
                 def to_device(device, array=array, there=there, send_sem=send_sem, recv_sem=recv_sem):
                     send(array.at[:, columns(device, head)], there, send_sem, recv_sem, device)
@@ -106,8 +105,9 @@
                     each_partner(chips - i, act)
                     return carry
 
+                lax.fori_loop(1, chips, to_chip, 0)
                 other_core(to_device)
-                lax.fori_loop(1, chips, to_chip, 0)
+                pltpu.make_async_copy(array.at[:, columns(me, head)], there, recv_sem).start()
         return carry
 
     lax.fori_loop(0, heads, start_head, 0)

time: 102 us -> 102 us (level)
  no operation moved by 1% of the time
where the time goes in v5:
time: 102 us
  Pallas kernels  101 us (99%)
    pallas_call x1, Pallas kernels, body(): pl.pallas_call(kernel, out_shape=(pltpu.VMEM((rows, width), BF16),) * 2,...  100 us

profile of v5, /device:TPU:1, one launch (start us, length us, event | category | flops | bytes accessed | tf_op | source)
XLA Modules:
  0.0 102.1 jit_solution(10674400678817382483)
XLA Ops:
  0.6 100.1 %attend_exchange.1 = (bf16[128,4096]{1,0:T(8,128)(2,1)S(1)}, bf16[128,4096]{1,0:T(8,128)(2,1)S(1)}) custom-call(bf16[128,4096]{1,0:T(8,128)(2,1)} %q_in.1, bf16[128,4096]{1,0:T(8,128)(2,1)} %k_in.1, bf16[128,4096]{1,0:T(8,128)(2,1)} %v_in.1, bf16[128,4096]{1,0:T(8,128)(2,1)} %dq_in.1, bf16[128,4096]{1,0:T(8,128)(2,1)} %dk_in.1, bf16[128,4096]{1,0:T(8,128)(2,1)} %dv_in.1), custom_call_target="tpu_custom_call" | custom-call | flops 12884901888 | bytes 8388608 | tf_op jit(solution)/shard_map/attend_exchange/pallas_call | solution.py:191
  100.7 1.3 %settle.1 = (bf16[128,4096]{1,0:T(8,128)(2,1)}, bf16[128,4096]{1,0:T(8,128)(2,1)}) custom-call(bf16[128,4096]{1,0:T(8,128)(2,1)S(1)} %get-tuple-element.4.a, bf16[128,4096]{1,0:T(8,128)(2,1)S(1)} %get-tuple-element.5.b), custom_call_target="tpu_custom_call" | custom-call | tf_op jit(solution)/shard_map/settle/pallas_call | solution.py:173

commit v6 on v5

--- a/solution.py
+++ b/solution.py
@@ -37,7 +37,7 @@
 
 def kernel(
     q_in, k_in, v_in, dq_in, dk_in, dv_in,
-    out, out_delta,
+    out,
     kv, qs, res,
     kv_send, kv_recv, q_send, q_recv, o_send, o_recv,
 ):
@@ -117,8 +117,7 @@
 
     def send_res(head, device):
         owned = pl.ds(pl.multiple_of(device * rows, rows), rows)
-        for i, array in enumerate((out, out_delta)):
-            send(res.at[head, i, owned, :], array.at[:, columns(me, head)], o_send, o_recv.at[i], device)
+        send(res.at[head, :, owned, :], out.at[:, :, columns(me, head)], o_send, o_recv, device)
 
     def step_chip(i, carry):
         head, step = i // chips, lax.rem(i, chips)
@@ -136,10 +135,9 @@
 
         @pl.when(step == 0)
         def _():
-            for j, array in enumerate((out, out_delta)):
-                pltpu.make_async_copy(
-                    res.at[head, j, mine, :], array.at[:, columns(me, head)], o_recv.at[j]
-                ).start()
+            pltpu.make_async_copy(
+                res.at[head, :, mine, :], out.at[:, :, columns(me, head)], o_recv
+            ).start()
             other_core(functools.partial(send_res, head))
 
         @pl.when(step != 0)
@@ -156,28 +154,27 @@
         drain(kv.at[head, :, others, :], kv_send.at[head])
         drain(qs.at[head, others, :], q_send.at[head])
     drain(res.at[:, :, others, :], o_send)
-    drain(out, o_recv.at[0])
-    drain(out_delta, o_recv.at[1])
-
-
-def settle_kernel(a, b, out_a, out_b, sems):
-    copies = [pltpu.make_async_copy(a, out_a, sems.at[0]), pltpu.make_async_copy(b, out_b, sems.at[1])]
+    drain(out, o_recv)
+
+
+def settle_kernel(both, out, out_delta, sems):
+    copies = [pltpu.make_async_copy(both.at[i], array, sems.at[i]) for i, array in enumerate((out, out_delta))]
     for copy in copies:
         copy.start()
     for copy in copies:
         copy.wait()
 
 
-def settle(a, b, space):
+def settle(both):
     anywhere = pl.BlockSpec(memory_space=pl.ANY)
     return pl.pallas_call(
         settle_kernel,
-        out_shape=(jax.ShapeDtypeStruct(a.shape, a.dtype),) * 2,
-        in_specs=[space] * 2,
+        out_shape=(jax.ShapeDtypeStruct(both.shape[1:], both.dtype),) * 2,
+        in_specs=[pl.BlockSpec(memory_space=pltpu.VMEM)],
         out_specs=(anywhere,) * 2,
         scratch_shapes=[pltpu.SemaphoreType.DMA((2,))],
         name="settle",
-    )(a, b)
+    )(both)
 
 
 def body(*arrays):
@@ -190,14 +187,14 @@
     products = 6 * 2 * tokens * tokens * HEAD_DIM * heads
     result = pl.pallas_call(
         kernel,
-        out_shape=(pltpu.VMEM((rows, width), BF16),) * 2,
+        out_shape=pltpu.VMEM((2, rows, width), BF16),
         in_specs=[anywhere] * 6,
-        out_specs=(pl.BlockSpec(memory_space=pltpu.VMEM),) * 2,
+        out_specs=pl.BlockSpec(memory_space=pltpu.VMEM),
         scratch_shapes=[
             pltpu.VMEM((heads, 2, tokens, 2 * HEAD_DIM), BF16),
             pltpu.VMEM((heads, tokens, 2 * HEAD_DIM), BF16),
             pltpu.VMEM((heads, 2, tokens, HEAD_DIM), BF16),
-            dma((heads,)), dma((heads,)), dma((heads,)), dma((heads, n // CORES)), dma, dma((2,)),
+            dma((heads,)), dma((heads,)), dma((heads,)), dma((heads, n // CORES)), dma, dma,
         ],
         compiler_params=pltpu.CompilerParams(
             collective_id=0, has_side_effects=True, vmem_limit_bytes=60 << 20
@@ -207,8 +204,7 @@
         ),
         name="attend_exchange",
     )(*arrays)
-    result = [pltpu.with_memory_space_constraint(r, pltpu.VMEM) for r in result]
-    return settle(*result, pl.BlockSpec(memory_space=pltpu.VMEM))
+    return settle(pltpu.with_memory_space_constraint(result, pltpu.VMEM))
 
 
 def solution(mesh):

time: 102 us -> 102 us (level)
  no operation moved by 1% of the time
where the time goes in v6:
time: 102 us
  Pallas kernels  101 us (99%)
    pallas_call x1, Pallas kernels, body(): pl.pallas_call(kernel, out_shape=pltpu.VMEM((2, rows, width), BF16), in_s...  100 us

profile of v6, /device:TPU:1, one launch (start us, length us, event | category | flops | bytes accessed | tf_op | source)
XLA Modules:
  0.0 102.0 jit_solution(4254156893967047810)
XLA Ops:
  0.6 100.1 %attend_exchange.1.both = bf16[2,128,4096]{2,1,0:T(8,128)(2,1)S(1)} custom-call(bf16[128,4096]{1,0:T(8,128)(2,1)} %q_in.1, bf16[128,4096]{1,0:T(8,128)(2,1)} %k_in.1, bf16[128,4096]{1,0:T(8,128)(2,1)} %v_in.1, bf16[128,4096]{1,0:T(8,128)(2,1)} %dq_in.1, bf16[128,4096]{1,0:T(8,128)(2,1)} %dk_in.1, bf16[128,4096]{1,0:T(8,128)(2,1)} %dv_in.1), custom_call_target="tpu_custom_call" | custom-call | flops 12884901888 | bytes 8388608 | tf_op jit(solution)/shard_map/attend_exchange/pallas_call | solution.py:188
  100.7 1.3 %settle.1 = (bf16[128,4096]{1,0:T(8,128)(2,1)}, bf16[128,4096]{1,0:T(8,128)(2,1)}) custom-call(bf16[2,128,4096]{2,1,0:T(8,128)(2,1)S(1)} %attend_exchange.1.both), custom_call_target="tpu_custom_call" | custom-call | tf_op jit(solution)/shard_map/settle/pallas_call | solution.py:170

commit v7 on v6

--- a/solution.py
+++ b/solution.py
@@ -94,20 +94,27 @@
             ((k_in, dk_in, v_in, dv_in), (kv.at[head, 0], kv.at[head, 1]), kv_send.at[head], kv_recv.at[head]),
             ((dq_in, q_in), (qs.at[head],), q_send.at[head], q_recv.at[head, me // CORES]),
         )
-        for arrays, pairs, send_sem, recv_sem in groups:
+        def start(arrays, pairs, send_sem, recv_sem):
+            def there(i):
+                return pairs[i // 2].at[mine, pl.ds(i % 2 * HEAD_DIM, HEAD_DIM)]
+
+            def to_device(device):
+                for i, array in enumerate(arrays):
+                    send(array.at[:, columns(device, head)], there(i), send_sem, recv_sem, device)
+
+            def to_chip(i, carry):
+                each_partner(chips - i, to_device)
+                return carry
+
+            lax.fori_loop(1, chips, to_chip, 0)
+            other_core(to_device)
             for i, array in enumerate(arrays):
-                there = pairs[i // 2].at[mine, pl.ds(i % 2 * HEAD_DIM, HEAD_DIM)]
-
-                def to_device(device, array=array, there=there, send_sem=send_sem, recv_sem=recv_sem):
-                    send(array.at[:, columns(device, head)], there, send_sem, recv_sem, device)
-
-                def to_chip(i, carry, act=to_device):
-                    each_partner(chips - i, act)
-                    return carry
-
-                lax.fori_loop(1, chips, to_chip, 0)
-                other_core(to_device)
-                pltpu.make_async_copy(array.at[:, columns(me, head)], there, recv_sem).start()
+                pltpu.make_async_copy(array.at[:, columns(me, head)], there(i), recv_sem).start()
+
+        (arrays, pairs, send_sem, recv_sem), queries = groups
+        for i in range(0, len(arrays), 2):
+            start(arrays[i : i + 2], pairs[i // 2 : i // 2 + 1], send_sem, recv_sem)
+        start(*queries)
         return carry
 
     lax.fori_loop(0, heads, start_head, 0)

time: 102 us -> 102 us (level)
  no operation moved by 1% of the time
where the time goes in v7:
time: 102 us
  Pallas kernels  102 us (100%)
    pallas_call x1, Pallas kernels, body(): pl.pallas_call(kernel, out_shape=pltpu.VMEM((2, rows, width), BF16), in_s...  100 us

profile of v7, /device:TPU:1, one launch (start us, length us, event | category | flops | bytes accessed | tf_op | source)
XLA Modules:
  0.0 102.3 jit_solution(4321657388417005730)
XLA Ops:
  0.6 100.4 %attend_exchange.1.both = bf16[2,128,4096]{2,1,0:T(8,128)(2,1)S(1)} custom-call(bf16[128,4096]{1,0:T(8,128)(2,1)} %q_in.1, bf16[128,4096]{1,0:T(8,128)(2,1)} %k_in.1, bf16[128,4096]{1,0:T(8,128)(2,1)} %v_in.1, bf16[128,4096]{1,0:T(8,128)(2,1)} %dq_in.1, bf16[128,4096]{1,0:T(8,128)(2,1)} %dk_in.1, bf16[128,4096]{1,0:T(8,128)(2,1)} %dv_in.1), custom_call_target="tpu_custom_call" | custom-call | flops 12884901888 | bytes 8388608 | tf_op jit(solution)/shard_map/attend_exchange/pallas_call | solution.py:195
  101.0 1.3 %settle.1 = (bf16[128,4096]{1,0:T(8,128)(2,1)}, bf16[128,4096]{1,0:T(8,128)(2,1)}) custom-call(bf16[2,128,4096]{2,1,0:T(8,128)(2,1)S(1)} %attend_exchange.1.both), custom_call_target="tpu_custom_call" | custom-call | tf_op jit(solution)/shard_map/settle/pallas_call | solution.py:177

commit v8 on v6

--- a/solution.py
+++ b/solution.py
@@ -102,7 +102,8 @@
                     send(array.at[:, columns(device, head)], there, send_sem, recv_sem, device)
 
                 def to_chip(i, carry, act=to_device):
-                    each_partner(chips - i, act)
+                    other_row_last = jnp.where(i == Z, Z, lax.rem(chips + Z - i, chips))
+                    each_partner(jnp.where(core == 0, chips - i, other_row_last), act)
                     return carry
 
                 lax.fori_loop(1, chips, to_chip, 0)

time: 102 us -> 102 us (level)
  no operation moved by 1% of the time
where the time goes in v8:
time: 102 us
  Pallas kernels  102 us (100%)
    pallas_call x1, Pallas kernels, body(): pl.pallas_call(kernel, out_shape=pltpu.VMEM((2, rows, width), BF16), in_s...  100 us

profile of v8, /device:TPU:1, one launch (start us, length us, event | category | flops | bytes accessed | tf_op | source)
XLA Modules:
  0.0 102.2 jit_solution(16496910786239290011)
XLA Ops:
  0.6 100.3 %attend_exchange.1.both = bf16[2,128,4096]{2,1,0:T(8,128)(2,1)S(1)} custom-call(bf16[128,4096]{1,0:T(8,128)(2,1)} %q_in.1, bf16[128,4096]{1,0:T(8,128)(2,1)} %k_in.1, bf16[128,4096]{1,0:T(8,128)(2,1)} %v_in.1, bf16[128,4096]{1,0:T(8,128)(2,1)} %dq_in.1, bf16[128,4096]{1,0:T(8,128)(2,1)} %dk_in.1, bf16[128,4096]{1,0:T(8,128)(2,1)} %dv_in.1), custom_call_target="tpu_custom_call" | custom-call | flops 12884901888 | bytes 8388608 | tf_op jit(solution)/shard_map/attend_exchange/pallas_call | solution.py:189
  100.9 1.3 %settle.1 = (bf16[128,4096]{1,0:T(8,128)(2,1)}, bf16[128,4096]{1,0:T(8,128)(2,1)}) custom-call(bf16[2,128,4096]{2,1,0:T(8,128)(2,1)S(1)} %attend_exchange.1.both), custom_call_target="tpu_custom_call" | custom-call | tf_op jit(solution)/shard_map/settle/pallas_call | solution.py:171
